TPU v7x, 256 devices: a whole 4x4x8 slice. The times are simulated.
256 devices in a mesh: cloud: 8 (over y_lo, x), leaf: 32 (over y_hi, z, core).
Axes of the slice: x: 4, y: 4 (y_hi: 2, y_lo: 2; y = y_hi * 2 + y_lo), z: 8, core: 2. Of those that a mesh axis runs over, the one named last changes fastest.
Arguments:
- points: bfloat16 [262144, 512], P(('cloud', 'leaf')), parts along dimension 0
- tree_order: int32 [262144], P(('cloud', 'leaf')), parts along dimension 0, may hold values from 0 to 1023, as said below
- present: int32 [262144], P(('cloud', 'leaf')), parts along dimension 0, may hold values 0 or 1
- gain_attn: float32 [3, 512], replicated, may hold values from 0.1 to 1.9
- query_weight: bfloat16 [3, 512, 512], replicated
- key_weight: bfloat16 [3, 512, 512], replicated
- value_weight: bfloat16 [3, 512, 512], replicated, may hold values from -0.25 to 0.25
- out_weight: bfloat16 [3, 512, 512], replicated, may hold values from -0.25 to 0.25
- gain_mlp: float32 [512], replicated, may hold values from 0.1 to 1.9
- hidden_weight: bfloat16 [512, 2048], replicated, may hold values from -0.25 to 0.25
- proj_weight: bfloat16 [2048, 512], replicated, may hold values from -0.125 to 0.125
Outputs:
- field: bfloat16 [262144, 512], P(('cloud', 'leaf')), parts along dimension 0
There are 8 independent parts, one for each index of `cloud`. A program takes and returns all parts, laid end to end along the dimension named above; an argument that names none is the same for every part. Nothing has to cross between parts.
Inputs may be any that keep to these rules, and one draw needn't show every extreme that they name: `tree_order`: within each aligned block of 1024 entries, each of 0 to 1023 appears once.
All inputs are finite; a program needn't handle non-finite values. No bound on the sum of `present` on one device may be relied on, other than what follows from the above.
Results may differ from a plain program's by a relative error of at most 0.025.
Values may be sent and summed in bfloat16 or wider, within the bound.
No kernel may reach another device: no remote copies, remote signals or barrier semaphores. Data moves between devices by JAX's collectives and lax.ppermute only.
A program may use at most 192 MiB of HBM per device.

v0:
```python
import functools
import jax
import jax.numpy as jnp
from jax import lax
from jax.experimental import pallas as pl
from jax.experimental.pallas import tpu as pltpu
from jax.sharding import PartitionSpec as P

D = 512
HEAD = 64
HEADS = 8
VROWS = 80
LIMIT2 = 60.0**2
QSCALE = HEAD ** (-0.5)
NT = (((1,), (1,)), ((), ()))
TN = (((0,), (0,)), ((), ()))
BF = jnp.bfloat16
F32 = jnp.float32
ANY = pl.BlockSpec(memory_space=pl.ANY)
VMEM = pl.BlockSpec(memory_space=pltpu.VMEM)
FLAT = 1024 * 576
SENT = (384, 224, 224, 192)
USUAL = sum(SENT[:-1])
EARLY = SENT[0]


def dotf(a, b, dims=(((1,), (0,)), ((), ()))):
    return lax.dot_general(a, b, dims, preferred_element_type=F32)


def norm_rows(values, gain):
    wide = values.astype(F32)
    centre = jnp.mean(wide, axis=-1, keepdims=True)
    wide = wide - centre
    spread = jnp.mean(jnp.square(wide), axis=-1, keepdims=True)
    return (wide * lax.rsqrt(spread + 1e-05) * gain).astype(BF)


def to_column(row):
    eye = lax.broadcasted_iota(jnp.int32, (128, 128), 0) == lax.broadcasted_iota(
        jnp.int32, (128, 128), 1
    )
    parts = []
    for start in range(0, row.shape[1], 128):
        block = jnp.where(eye, row[:, start : start + 128], 0.0)
        parts.append(jnp.sum(block, axis=1, keepdims=True))
    return jnp.concatenate(parts, axis=0)


def head_select():
    lane = lax.broadcasted_iota(jnp.int32, (16, D), 1)
    head = lax.broadcasted_iota(jnp.int32, (16, D), 0)
    return jnp.where(lane // HEAD == head, 1.0, 0.0).astype(BF)


def head_peak(rows):
    wide = rows.astype(F32)
    sums = dotf(head_select(), (wide * wide).astype(BF), NT)
    return jnp.broadcast_to(jnp.max(sums, axis=1, keepdims=True), (16, 128))


def split_queries(queries, q_ref):
    low = lax.broadcasted_iota(jnp.int32, (1, 128), 1) < HEAD
    for pair in range(HEADS // 2):
        part = queries[:, pair * 128 : (pair + 1) * 128]
        q_ref[2 * pair] = jnp.where(low, part, jnp.zeros_like(part))
        q_ref[2 * pair + 1] = jnp.where(low, jnp.zeros_like(part), part)


def fill_rows(fill_row):
    first = lax.broadcasted_iota(jnp.int32, (16, fill_row.shape[1]), 0) == 0
    return jnp.where(first, fill_row, 0.0).astype(BF)


def attend(q_ref, k_ref, vt_ref, ones_ref, o_ref, add_ref):
    count = k_ref.shape[0]
    blocks = [(start, min(256, count - start)) for start in range(0, count, 256)]
    depth = 2 if q_ref.shape[1] > 256 else 3

    def run(pairs, columns):
        waiting, totals = [], {}

        def drain():
            pair, head, block, scores = waiting.pop(0)
            start, size = block
            weights = jnp.exp(scores).astype(BF)
            keys = slice(start, start + size)
            values = vt_ref[columns(2 * pair + head, HEAD), keys]
            part = dotf(jnp.concatenate([values, ones_ref[:, keys]], axis=0), weights)
            total = totals.pop(head, None)
            total = part if total is None else total + part
            if block == blocks[-1]:
                if add_ref is not None:
                    total = total + add_ref[pair * 2 + head]
                o_ref[pair * 2 + head] = total
            else:
                totals[head] = total

        for pair in pairs:
            for head in range(2):
                queries = q_ref[2 * pair + head]
                for block in blocks:
                    start, size = block
                    keys = k_ref[start : start + size, columns(pair, 128)]
                    waiting.append((pair, head, block, dotf(keys, queries, NT)))
                    if len(waiting) > depth:
                        drain()
        while waiting:
            drain()

    if q_ref.shape[1] * count <= FLAT:
        run(range(HEADS // 2), lambda at, size: slice(at * size, (at + 1) * size))
        return

    def body(pair, carry):
        run([pair], lambda at, size: pl.ds(pl.multiple_of(at * size, size), size))
        return carry

    lax.fori_loop(0, HEADS // 2, body, 0)


def project_kv(normed, kw, vw, fill_row=None):
    keys = dotf(normed, kw.here[...]).astype(BF)
    values_t = dotf(vw.here[...], normed, (((0,), (1,)), ((), ())))
    if fill_row is not None:
        values_t = values_t * fill_row
    return keys, values_t.astype(BF)


def front_kernel(first, points, present, *outs):
    fill = present.here[...].astype(F32)
    upto = lax.broadcasted_iota(jnp.int32, (1024, 1024), 0) <= lax.broadcasted_iota(
        jnp.int32, (1024, 1024), 1
    )
    f8 = jnp.broadcast_to(fill, (8, 1024)).astype(BF)
    rank = dotf(f8, jnp.where(upto, 1.0, 0.0).astype(BF))[:1]
    place = jnp.where(fill > 0.0, rank - 1.0, -1.0).astype(jnp.int32)
    at = sum(SENT[:first])
    for out, count in zip(outs, SENT[first:]):
        rows = lax.broadcasted_iota(jnp.int32, (count, 1024), 0) + at
        pick = jnp.where(rows == place, 1.0, 0.0).astype(BF)
        out.ref[:count, :] = dotf(pick, points.here[...]).astype(BF)
        if at == 0:
            lane = lax.broadcasted_iota(jnp.int32, (16, D), 1)
            line = lax.broadcasted_iota(jnp.int32, (16, D), 0)
            total = jnp.broadcast_to(rank[:, 1023:], (16, D)).astype(jnp.int32)
            out.ref[count:, :] = jnp.where(line * D + lane < total, 1.0, 0.0).astype(BF)
        out.flush()
        at += count


def pooled_places(order_row):
    lanes = lax.broadcasted_iota(jnp.int32, (1024, 1024), 1).astype(F32)
    chosen = jnp.where(to_column(order_row) == lanes, 1.0, 0.0).astype(BF)
    row = lax.broadcasted_iota(jnp.int32, (8, 1024), 1)
    line = lax.broadcasted_iota(jnp.int32, (8, 1024), 0)
    both = dotf(jnp.where(line == 0, row // 4, (row // 2) % 2).astype(F32).astype(BF), chosen)
    return both[:1] + 256.0 * both[1:2]


def local_kernel(level, rows, x, fill_src, gains, qw, kw, vw, *refs):
    if level == 0:
        order, q, o, qp, kp, spot, k_ref, vt_ref, ones_ref = refs
        spot.ref[...] = jnp.broadcast_to(pooled_places(order.here[...].astype(F32)), (8, 1024))
        spot.flush()
    else:
        q, o, qp, kp, k_ref, vt_ref, ones_ref = refs
    normed = norm_rows(x.here[:rows, :], gains.here[level : level + 1, :])
    if level == 0:
        fill = fill_src.here[...].astype(F32)
        normed = normed * to_column(fill).astype(BF)
    else:
        fill = x.here[rows : rows + 1, :rows].astype(F32)
    queries = dotf(normed, qw.here[...]).astype(BF) * QSCALE
    split_queries(queries, q.ref)
    q.flush()
    keys, values_t = project_kv(normed, kw, vw)
    qp.ref[...] = head_peak(queries)
    kp.ref[...] = head_peak(keys)
    qp.flush()
    kp.flush()
    k_ref[...] = keys
    vt_ref[...] = (values_t.astype(F32) * fill).astype(BF)
    ones_ref[...] = fill_rows(fill)
    attend(q.ref, k_ref, vt_ref, ones_ref, o.ref, None)
    if level == 0:
        for head in range(HEADS):
            o.ref[head, HEAD : HEAD + 1, :] += 1.0 - fill
    else:
        prod = queries.astype(F32) * keys.astype(F32)
        high = prod.astype(BF)
        rest = (prod - high.astype(F32)).astype(BF)
        select = head_select()
        own = jnp.exp(dotf(select, high, NT) + dotf(select, rest, NT))
        own = own * (1.0 - fill)
        for head in range(HEADS):
            weight = own[head : head + 1]
            part = values_t[head * HEAD : (head + 1) * HEAD].astype(F32)
            o.ref[head, :HEAD, :] += part * weight
            o.ref[head, HEAD : HEAD + 1, :] += weight
    o.flush()


def far_fill(packed):
    at = packed.shape[0] - 16
    return jnp.concatenate([packed[at : at + 1, :], packed[at + 1 : at + 2, :]], axis=1).astype(F32)


def remote_kernel(first, gains, kw, vw, q, o_in, kp_in, mine, o, kp, over, k_ref, vt_ref,
                  ones_ref):
    normed = norm_rows(first.here[:EARLY, :], gains.here[0:1, :])
    fill = far_fill(first.here)[:, :EARLY]
    keys, values_t = project_kv(normed, kw, vw, fill)
    k_ref[...] = keys
    vt_ref[...] = values_t
    ones_ref[...] = fill_rows(fill)
    kp.ref[...] = jnp.maximum(kp_in.here[...], head_peak(keys))
    kp.flush()
    used = far_fill(first.here) + far_fill(mine.here)
    over.ref[...] = jnp.broadcast_to(used[:, USUAL : USUAL + 1], (8, 128)).astype(jnp.int32)
    over.flush()
    attend(q.here, k_ref, vt_ref, ones_ref, o.ref, o_in.here)
    o.flush()


def exact_attend(level, q_ref, own, fills, chunks, counts, gains, kw, vw, att_ref, xbuf, kf, vf):
    rows = q_ref.shape[1]
    for side, sources in enumerate(([(own, rows)], list(zip(chunks, counts)))):
        at = 0
        for ref, count in sources:
            pltpu.sync_copy(ref.at[pl.ds(0, count), :], xbuf.at[pl.ds(at, count), :])
            at += count
        for start in range(0, rows, 128):
            normed = norm_rows(xbuf[start : start + 128, :], gains.here[level : level + 1, :])
            if level == 0 and side == 0:
                normed = normed * to_column(fills[0][:, start : start + 128]).astype(BF)
            keys, values_t = project_kv(normed, kw, vw)
            base = side * rows + start
            kf[base : base + 128, :] = keys
            vf[:, base : base + 128] = values_t
    total = 2 * rows
    fill8 = jnp.broadcast_to(jnp.concatenate(fills, axis=1), (8, total)).astype(BF)
    width = 128

    def body(step, carry):
        pair = step // (rows // width)
        start = pl.multiple_of(step % (rows // width) * width, width)
        lanes = pl.ds(pl.multiple_of(pair * 128, 128), 128)
        keys = kf[:, lanes]
        mask = dotf(fill8, jnp.ones((8, width), BF), TN) > 0.5
        own = lax.broadcasted_iota(jnp.int32, (total, width), 0) == (
            lax.broadcasted_iota(jnp.int32, (total, width), 1) + start
        )
        allowed = mask | own
        for head in range(2):
            queries = q_ref[2 * pair + head, pl.ds(start, width), :]
            scores = jnp.where(allowed, dotf(keys, queries, NT), -1e30)
            weights = jnp.exp(scores - jnp.max(scores, axis=0, keepdims=True))
            weights = weights / jnp.sum(weights, axis=0, keepdims=True)
            first = pl.multiple_of(pair * 128 + head * HEAD, HEAD)
            values = vf[pl.ds(first, HEAD), :]
            att_ref[pl.ds(first, HEAD), pl.ds(start, width)] = dotf(
                values, weights.astype(BF)
            ).astype(BF)
        return carry

    lax.fori_loop(0, HEADS // 2 * (rows // width), body, 0)


def finish_attention(level, far, chunk_refs, counts, operands, scratch, fill, fill_far, rest=None):
    gains, kw, vw, q, qp, kp, o, own = operands
    att_ref, k_ref, vt_ref, ones_ref, xbuf, kf, vf = scratch[:7]
    gain = gains.here[level : level + 1, :]
    begin = 0 if rest is None else EARLY
    usual = begin + k_ref.shape[0]
    normed = [norm_rows(x.here[:count, :], gain) for x, count in zip(far, counts)]
    normed = jnp.concatenate(normed, axis=0) if len(normed) > 1 else normed[0]
    keys, values_t = project_kv(normed, kw, vw, fill_far[:, begin:usual])
    k_ref[...] = keys
    vt_ref[...] = values_t
    ones_ref[...] = fill_rows(fill_far[:, begin:usual])
    attend(q.here, k_ref, vt_ref, ones_ref, o.here, o.here)
    peak = jnp.maximum(kp.here[...], head_peak(keys)) * qp.here[...]
    own.here
    if rest is not None:
        rest_k, rest_vt, rest_ones, rest_peak = scratch[7:]
        rest_peak[...] = jnp.zeros_like(rest_peak)
        rest.here

        @pl.when(jnp.max(fill_far[:, usual:]) > 0.0)
        def _():
            keys, values_t = project_kv(
                norm_rows(rest.here[...], gain), kw, vw, fill_far[:, usual:])
            rest_k[...] = keys
            rest_vt[...] = values_t
            rest_ones[...] = fill_rows(fill_far[:, usual:])
            rest_peak[...] = head_peak(keys)
            attend(q.here, rest_k, rest_vt, rest_ones, o.here, o.here)

        peak = jnp.maximum(peak, rest_peak[...] * qp.here[...])
    for head in range(HEADS):
        scale = 1.0 / o.here[head, HEAD : HEAD + 1, :]
        att_ref[head * HEAD : (head + 1) * HEAD, :] = (o.here[head, :HEAD, :] * scale).astype(BF)
    inside = jnp.max(peak) <= LIMIT2

    @pl.when(jnp.logical_not(inside))
    def _():
        exact_attend(level, q.here, own.here, [fill, fill_far], chunk_refs,
                     counts if rest is None else SENT, gains, kw, vw, att_ref, xbuf, kf, vf)

    return att_ref[...]


def finish0_kernel(*refs):
    chunks = refs[: len(SENT)]
    (packed, second, third, fill_ref, gains, kw, vw, q, o, qp, kp, ow, points, tree, rest,
     y_out, x1_out) = refs[len(SENT) : len(SENT) + 17]
    scratch = refs[len(SENT) + 17 :]
    fill = fill_ref.here[...].astype(F32)
    attended_t = finish_attention(
        0, [second, third], chunks, SENT[1:3], (gains, kw, vw, q, qp, kp, o, points), scratch,
        fill, far_fill(packed.here), rest)
    x0 = points.here[...].astype(F32) * to_column(fill)
    y = (x0 + dotf(attended_t, ow.here[...], TN)).astype(BF)
    y_out.ref[...] = y
    y_out.flush()
    f8 = jnp.broadcast_to(fill, (8, 1024)).astype(BF)
    place = tree.here[:1, :]
    fills = []
    for half in range(2):
        rows = (lax.broadcasted_iota(jnp.int32, (256, 1024), 0) + 256 * half).astype(F32)
        pool = jnp.where(rows == place, 0.5, 0.0).astype(BF)
        x1_out.ref[half * 256 : (half + 1) * 256, :] = dotf(pool, y).astype(BF)
        fills.append(jnp.where(dotf(f8, pool, NT)[:1] > 0.25, 1.0, 0.0))
    x1_out.ref[512:, :] = jnp.broadcast_to(jnp.concatenate(fills, axis=1), (16, D)).astype(BF)
    x1_out.flush()


def finish1_kernel(far_hbm, last, gains, kw, vw, q, o_in, qp, kp, x, ow, y_out, x2_out, *scratch):
    fill = x.here[512:513, :].astype(F32)
    attended_t = finish_attention(
        1, [last], [far_hbm], (512,), (gains, kw, vw, q, qp, kp, o_in, x), scratch, fill,
        last.here[512:513, :].astype(F32))
    y = (x.here[:512, :].astype(F32) + dotf(attended_t, ow.here[...], TN)).astype(BF)
    wide = y.astype(F32)
    x2_out.ref[:256, :] = ((wide[:256] + wide[256:]) * 0.5).astype(BF)
    f_next = jnp.maximum(fill[:, :256], fill[:, 256:])
    x2_out.ref[256:, :] = jnp.broadcast_to(
        jnp.concatenate([f_next, f_next], axis=1), (16, D)).astype(BF)
    x2_out.flush()
    y_out.ref[...] = y
    y_out.flush()


def finish2_kernel(far_hbm, last, gains, kw, vw, q, o_in, qp, kp, x, ow, gm, hw, pw, y1, y0, tree,
                   field, *scratch):
    fill = x.here[256:257, :256].astype(F32)
    attended_t = finish_attention(
        2, [last], [far_hbm], (256,), (gains, kw, vw, q, qp, kp, o_in, x), scratch, fill,
        last.here[256:257, :256].astype(F32))
    y2 = (x.here[:256, :].astype(F32) + dotf(attended_t, ow.here[...], TN)).astype(BF)
    normed = norm_rows(y2, gm.here[...])
    hw.here, pw.here
    total = y2.astype(F32)
    before = None
    for start in range(0, 2048 + 512, 512):
        if start < 2048:
            now = dotf(normed, hw.here[:, start : start + 512])
        if before is not None:
            hidden = jax.nn.gelu(before, approximate=True).astype(BF)
            total = total + dotf(hidden, pw.here[start - 512 : start, :])
        before = now
    top = total.astype(BF).astype(F32)
    up = [(y1.here[half * 256 : (half + 1) * 256, :].astype(F32) + top).astype(BF)
          for half in range(2)]
    place = to_column(tree.here[:1, :])
    lanes = lax.broadcasted_iota(jnp.int32, (256, 256), 1).astype(F32)
    for side, out in enumerate(field.parts(4)):
        total = y0.here[256 * side : 256 * (side + 1), :].astype(F32)
        for half in range(2):
            picked = place[256 * side : 256 * (side + 1)] == lanes + 256.0 * half
            total = total + dotf(jnp.where(picked, 1.0, 0.0).astype(BF), up[half])
        field.ref[256 * side : 256 * (side + 1), :] = total.astype(BF)
        out.start()


class Here:
    def __init__(self, ref, copy=None):
        self.here = self.ref = ref
        self.copy = copy

    def flush(self):
        if self.copy is not None:
            self.copy.start()

    def parts(self, count):
        rows = self.ref.shape[0] // count
        source, target, sem = self.ends
        return [
            pltpu.make_async_copy(
                source.at[pl.ds(i * rows, rows), :], target.at[pl.ds(i * rows, rows), :], sem)
            for i in range(count)
        ]


class Piece:
    def __init__(self, copy, ref):
        self.copy, self.ref = copy, ref

    @property
    def here(self):
        if self.copy is not None:
            self.copy.wait()
            self.copy = None
        return self.ref


def call(kernel, outs, args, raw=(), scratch=(), flops=0, limit=64, manual=False, away=()):
    arrays = [a[0] if isinstance(a, tuple) else a for a in args]
    n, m = len(args), len(outs)
    moved = [i for i in range(n) if isinstance(args[i], tuple) or (manual and i not in raw)]
    level = [args[i][1] if isinstance(args[i], tuple) else None for i in range(n)]
    buffers = [
        pltpu.VMEM(arrays[i].shape if level[i] is None else arrays[i].shape[1:], arrays[i].dtype)
        for i in moved
    ]
    away = list(range(m)) if manual else sorted(away)
    sems = [pltpu.SemaphoreType.DMA((len(moved),))] if moved else []
    if away:
        buffers = [pltpu.VMEM(outs[i].shape, outs[i].dtype) for i in away] + buffers
        sems.append(pltpu.SemaphoreType.DMA((m,)))

    def body(*refs):
        sources, targets, rest = refs[:n], refs[n : n + m], list(refs[n + m :])
        results = [Here(t) for t in targets]
        held, rest = rest[: len(away)], rest[len(away) :]
        slots, rest = rest[: len(moved)], rest[len(moved) :]
        operands = [s if i in raw else Here(s) for i, s in enumerate(sources)]
        if moved:
            sem = rest.pop(0)
        if away:
            out_sem = rest.pop(0)
        for i, h in zip(away, held):
            results[i] = Here(h, pltpu.make_async_copy(h, targets[i], out_sem.at[i]))
            results[i].ends = (h, targets[i], out_sem.at[i])
        for slot, i in enumerate(moved):
            source = sources[i] if level[i] is None else sources[i].at[level[i]]
            copy = pltpu.make_async_copy(source, slots[slot], sem.at[slot])
            copy.start()
            operands[i] = Piece(copy, slots[slot])
        kernel(*operands, *results, *rest)
        for i in moved:
            operands[i].here
        for i in away:
            results[i].copy.wait()

    nbytes = sum(a.size * a.dtype.itemsize for a in arrays) + sum(
        a.size * a.dtype.itemsize for a in outs)
    return pl.pallas_call(
        body,
        out_shape=outs,
        in_specs=[ANY if manual or i in raw or i in moved else VMEM for i in range(n)],
        out_specs=[ANY if i in away else VMEM for i in range(m)],
        scratch_shapes=buffers + sems + list(scratch),
        compiler_params=pltpu.CompilerParams(vmem_limit_bytes=limit * 2**20),
        cost_estimate=pl.CostEstimate(flops=flops, bytes_accessed=nbytes, transcendentals=0),
    )(*arrays)


def shape(*dims, dtype=BF):
    return jax.ShapeDtypeStruct(dims, dtype)


def key_scratch(rows):
    return [pltpu.VMEM((rows, D), BF), pltpu.VMEM((D, rows), BF), pltpu.VMEM((16, rows), BF)]


def local_part(level, x, fill, gains, qw, kw, vw, rows, manual, order=()):
    return call(
        functools.partial(local_kernel, level, rows),
        [shape(HEADS, rows, 128), shape(HEADS, VROWS, rows, dtype=F32),
         shape(16, 128, dtype=F32), shape(16, 128, dtype=F32)]
        + [shape(8, rows, dtype=F32) for _ in order],
        [x, fill, gains, (qw, level), (kw, level), (vw, level), *order],
        scratch=key_scratch(rows),
        flops=8 * rows * rows * 512 * 2,
        manual=manual,
        limit={0: 64, 1: 16, 2: 12}[level],
    )


def finish_part(kernel, args, raw, outs, rows, count, manual, extra=(), away=()):
    return call(
        kernel,
        outs,
        args,
        raw=set(range(raw)),
        scratch=[
            pltpu.VMEM((D, rows), BF),
            *key_scratch(count),
            pltpu.VMEM((rows, D), BF),
            pltpu.VMEM((2 * rows, D), BF),
            pltpu.VMEM((D, 2 * rows), BF),
            *extra,
        ],
        flops=8 * rows * count * 512 * 2 + 4 * rows * D * D,
        manual=manual,
        away=away,
        limit={1024: 64, 512: 16, 256: 24}[rows],
    )


def per_device(points, tree_order, present, gain_attn, query_weight, key_weight, value_weight,
               out_weight, gain_mlp, hidden_weight, proj_weight):
    size = lax.axis_size("leaf")

    def trade(value, bit):
        return lax.ppermute(value, "leaf", [(s, s ^ (1 << bit)) for s in range(size)])

    base = size.bit_length() - 1 - 3
    fill0 = present.reshape(1, 1024)
    parts = []
    for first, last in ((0, 1), (1, len(SENT))):
        parts += call(
            functools.partial(front_kernel, first),
            [shape(count + (0 if first else 16), D) for count in SENT[first:last]],
            [points, fill0], flops=10**9, manual=True)
    chunks = [trade(part, base) for part in parts[:-1]]

    def kvs(level):
        return [(key_weight, level), (value_weight, level)]

    q, o, qp, kp, spot = local_part(0, points, fill0, gain_attn, query_weight, key_weight,
                                    value_weight, 1024, True, [tree_order.reshape(1, 1024)])
    o, kp, over = call(
        remote_kernel,
        [shape(HEADS, VROWS, 1024, dtype=F32), shape(16, 128, dtype=F32),
         shape(8, 128, dtype=jnp.int32)],
        [chunks[0], gain_attn, *kvs(0), q, o, kp, parts[0]],
        scratch=key_scratch(EARLY), flops=10**10, manual=True)
    chunks.append(lax.cond(
        over[0, 0] > 0, lambda left: trade(left, base), lambda left: left, parts[-1]))
    y0, x1 = finish_part(
        finish0_kernel,
        [*chunks, *chunks[:3], fill0, gain_attn, *kvs(0), q, o, qp, kp, (out_weight, 0), points,
         spot, chunks[3]],
        len(SENT), [shape(1024, D), shape(528, D)], 1024, USUAL - EARLY, True,
        extra=[*key_scratch(SENT[-1]), pltpu.VMEM((16, 128), F32)])
    far1 = trade(x1, base + 1)
    q, o, qp, kp = local_part(1, x1, fill0, gain_attn, query_weight, key_weight, value_weight,
                              512, False)
    y1, x2 = finish_part(
        finish1_kernel,
        [far1, far1, gain_attn, *kvs(1), q, o, qp, kp, x1, (out_weight, 1)],
        1, [shape(512, D), shape(272, D)], 512, 512, False, away={0, 1})
    far2 = trade(x2, base + 2)
    q, o, qp, kp = local_part(2, x2, fill0, gain_attn, query_weight, key_weight, value_weight,
                              256, True)
    (field,) = finish_part(
        finish2_kernel,
        [far2, far2, gain_attn, *kvs(2), q, o, qp, kp, x2, (out_weight, 2),
         gain_mlp.reshape(1, D), (hidden_weight, None), (proj_weight, None), y1, y0, spot],
        1, [shape(1024, D)], 256, 256, True)
    return field


def solution(mesh):
    placed = (
        P(("cloud", "leaf"), None),
        P(("cloud", "leaf")),
        P(("cloud", "leaf")),
        P(), P(), P(), P(), P(), P(), P(), P(),
    )
    return jax.shard_map(
        per_device,
        mesh=mesh,
        in_specs=placed,
        out_specs=P(("cloud", "leaf"), None),
        check_vma=False,
    )
```

profile of v0, /device:TPU:18, one launch (start us, length us, event | category | flops | bytes accessed | tf_op | source)
XLA Modules:
  0.0 209.7 jit_solution(16692420872775052124)
XLA Ops:
  0.0 2.9 %shard_map.109.refs_7_ = bf16[400,512]{1,0:T(8,128)(2,1)} custom-call(bf16[1024,512]{1,0:T(8,128)(2,1)} %refs_16_.1, s32[1,1024]{1,0:T(1,128)} %bitcast.4), custom_call_target="tpu_custom_call" | custom-call | flops 1000000000 | bytes 1462272 | tf_op jit(solution)/shard_map/pallas_call | solution.py:459
  2.9 3.4 %collective-permute-start.1 = (bf16[400,512]{1,0:T(8,128)(2,1)}, bf16[400,512]{1,0:T(8,128)(2,1)}, u32[]{:S(2)}, u32[]{:S(2)}) collective-permute-start(bf16[400,512]{1,0:T(8,128)(2,1)} %shard_map.109.refs_7_), channel_id=1, source_target_pairs={{0,4},{1,5},{2,6},{3,7},{4,0},{5,1},{6,2},{7,3},{8,12},{9,13},{10,... | collective-permute-start | bytes 1228808 | tf_op jit(solution)/shard_map/ppermute | solution.py:518
  6.3 2.9 %shard_map.110 = (bf16[224,512]{1,0:T(8,128)(2,1)}, bf16[224,512]{1,0:T(8,128)(2,1)}, bf16[192,512]{1,0:T(8,128)(2,1)}) custom-call(bf16[1024,512]{1,0:T(8,128)(2,1)} %refs_16_.1, s32[1,1024]{1,0:T(1,128)} %bitcast.5), custom_call_target="tpu_custom_call" | custom-call | flops 1000000000 | bytes 1708032 | tf_op jit(solution)/shard_map/pallas_call | solution.py:459
  9.2 0.1 collective-permute-start.2
  9.3 3.1 %collective-permute-start.3 = (bf16[224,512]{1,0:T(8,128)(2,1)}, bf16[224,512]{1,0:T(8,128)(2,1)}, u32[]{:S(2)}, u32[]{:S(2)}) collective-permute-start(bf16[224,512]{1,0:T(8,128)(2,1)} %get-tuple-element.34), channel_id=1, source_target_pairs={{0,4},{1,5},{2,6},{3,7},{4,0},{5,1},{6,2},{7,3},{8,12},{9,13},{10,... | collective-permute-start | bytes 688136 | tf_op jit(solution)/shard_map/ppermute | solution.py:518
  12.4 15.8 %shard_map.111 = (bf16[8,1024,128]{2,1,0:T(8,128)(2,1)}, f32[8,80,1024]{2,1,0:T(8,128)}, f32[16,128]{1,0:T(8,128)}, f32[16,128]{1,0:T(8,128)}, f32[8,1024]{1,0:T(8,128)}) custom-call(bf16[1024,512]{1,0:T(8,128)(2,1)} %refs_16_.1, s32[1,1024]{1,0:T(1,128)} %bitcast.6, f32[3,512]{1,0:T(4,128)} %refs_2_.11, bf16[3,512,512]{2,1,0:T(8,128)(2,1)} %refs_3_.10, ...), custom_call_target="tpu_custom_call" | custom-call | flops 8589934592 | bytes 10549248 | tf_op jit(solution)/shard_map/pallas_call | solution.py:459
  28.2 7.3 %collective-permute-done.1.refs_0_.refs_4_ = bf16[400,512]{1,0:T(8,128)(2,1)} collective-permute-done((bf16[400,512]{1,0:T(8,128)(2,1)}, bf16[400,512]{1,0:T(8,128)(2,1)}, u32[]{:S(2)}, u32[]{:S(2)}) %collective-permute-start.1) | collective-permute-done | bytes 409632 | tf_op jit(solution)/shard_map/ppermute | solution.py:518
  35.5 7.7 %shard_map.112 = (f32[8,80,1024]{2,1,0:T(8,128)}, f32[16,128]{1,0:T(8,128)}, s32[8,128]{1,0:T(8,128)}) custom-call(bf16[400,512]{1,0:T(8,128)(2,1)} %collective-permute-done.1.refs_0_.refs_4_, f32[3,512]{1,0:T(4,128)} %refs_2_.11, bf16[3,512,512]{2,1,0:T(8,128)(2,1)} %refs_3_.11, bf16[3,512,512]{2,1,0:T(8,128)(2,1)} %refs_4_.9, ...), custom_call_target="tpu_custom_call" | custom-call | flops 10000000000 | bytes 11331584 | tf_op jit(solution)/shard_map/pallas_call | solution.py:459
  43.2 1.2 slice.3
  45.0 0.3 conditional.1
  45.3 0.0 collective-permute-done.2.refs_1_.refs_5_
  45.3 0.0 collective-permute-done.3.refs_2_.refs_6_
  45.3 84.9 %shard_map.113 = (bf16[1024,512]{1,0:T(8,128)(2,1)}, bf16[528,512]{1,0:T(8,128)(2,1)}) custom-call(bf16[400,512]{1,0:T(8,128)(2,1)} %collective-permute-done.1.refs_0_.refs_4_, bf16[224,512]{1,0:T(8,128)(2,1)} %collective-permute-done.2.refs_1_.refs_5_, bf16[224,512]{1,0:T(8,128)(2,1)} %collective-permute-done.3.refs_2_.refs_6_, ...), custom_call_target="tpu_custom_call" | custom-call | flops 4831838208 | bytes 14264320 | tf_op jit(solution)/shard_map/pallas_call | solution.py:459
  130.2 6.6 %collective-permute-start.4 = (bf16[528,512]{1,0:T(8,128)(2,1)}, bf16[528,512]{1,0:T(8,128)(2,1)S(1)}, u32[]{:S(2)}, u32[]{:S(2)}) collective-permute-start(bf16[528,512]{1,0:T(8,128)(2,1)} %get-tuple-element.44.refs_0_.refs_9_), channel_id=1, source_target_pairs={{0,8},{1,9},{2,10},{3,11},{4,12},{5,13},{6,14},{7,15},{8,0},{9,1},... | collective-permute-start | bytes 1622024 | tf_op jit(solution)/shard_map/ppermute | solution.py:518
  136.7 0.0 copy-start
  136.7 1.4 copy-done
  138.1 0.0 copy-start.2
  138.1 1.4 copy-done.2
  139.6 0.0 copy-start.7
  139.6 1.4 copy-done.7
  141.0 0.0 copy-start.11
  141.0 0.7 copy-done.11
  141.7 0.0 copy-start.13
  141.7 0.7 copy-done.13
  142.3 0.0 copy-start.15
  142.4 1.0 copy-done.15
  143.4 0.0 copy-start.1
  143.4 0.0 copy-start.3
  143.4 0.0 copy-start.6
  143.4 4.6 %shard_map.114 = (bf16[8,512,128]{2,1,0:T(8,128)(2,1)S(1)}, f32[8,80,512]{2,1,0:T(8,128)S(1)}, f32[16,128]{1,0:T(8,128)S(1)}, f32[16,128]{1,0:T(8,128)S(1)}) custom-call(bf16[528,512]{1,0:T(8,128)(2,1)S(1)} %copy-done.15, s32[1,1024]{1,0:T(1,128)S(1)} %bitcast.8, f32[3,512]{1,0:T(4,128)S(1)} %copy-done.11, bf16[3,512,512]{2,1,0:T(8,128)(2,1)S(1)} %copy-done.7, ...), custom_call_target="tpu_custom_call" | custom-call | flops 2147483648 | bytes 7645184 | tf_op jit(solution)/shard_map/pallas_call | solution.py:459
  148.1 12.1 %collective-permute-done.4.refs_0_.refs_1_ = bf16[528,512]{1,0:T(8,128)(2,1)S(1)} collective-permute-done((bf16[528,512]{1,0:T(8,128)(2,1)}, bf16[528,512]{1,0:T(8,128)(2,1)S(1)}, u32[]{:S(2)}, u32[]{:S(2)}) %collective-permute-start.4) | collective-permute-done | bytes 540704 | tf_op jit(solution)/shard_map/ppermute | solution.py:518
  160.1 0.0 copy-done.1
  160.1 0.0 copy-done.3
  160.1 0.0 copy-done.6
  160.1 0.0 copy-start.8
  160.1 0.0 copy-start.9
  160.1 26.6 %shard_map.115 = (bf16[512,512]{1,0:T(8,128)(2,1)S(1)}, bf16[272,512]{1,0:T(8,128)(2,1)S(1)}) custom-call(bf16[528,512]{1,0:T(8,128)(2,1)S(1)} %collective-permute-done.4.refs_0_.refs_1_, bf16[528,512]{1,0:T(8,128)(2,1)S(1)} %collective-permute-done.4.refs_0_.refs_1_, f32[3,512]{1,0:T(4,128)S(1)} %copy-done.11, bf16[3,512,512]{2,1,0:T(8,128)(2,1)S(1)} %copy-done.1, ...), custom_call_target="tpu_custom_call" | custom-call | flops 2684354560 | bytes 9525248 | tf_op jit(solution)/shard_map/pallas_call | solution.py:459
  186.8 0.0 copy-start.4
  186.8 0.0 copy-start.5
  186.8 0.0 copy-start.10
  186.8 0.0 copy-start.12
  186.8 0.0 copy-start.14
  186.8 0.6 collective-permute-start.5
  187.5 0.0 copy-done.8
  187.5 3.0 %shard_map.116 = (bf16[8,256,128]{2,1,0:T(8,128)(2,1)S(1)}, f32[8,80,256]{2,1,0:T(8,128)S(1)}, f32[16,128]{1,0:T(8,128)S(1)}, f32[16,128]{1,0:T(8,128)S(1)}) custom-call(bf16[272,512]{1,0:T(8,128)(2,1)S(1)} %get-tuple-element.49.refs_0_.refs_9_, s32[1,1024]{1,0:T(1,128)S(1)} %bitcast.9, f32[3,512]{1,0:T(4,128)S(1)} %copy-done.11, ...), custom_call_target="tpu_custom_call" | custom-call | flops 536870912 | bytes 6203392 | tf_op jit(solution)/shard_map/pallas_call | solution.py:459
  190.5 5.0 %collective-permute-done.5.refs_0_.refs_1_ = bf16[272,512]{1,0:T(8,128)(2,1)S(1)} collective-permute-done((bf16[272,512]{1,0:T(8,128)(2,1)S(1)}, bf16[272,512]{1,0:T(8,128)(2,1)S(1)}, u32[]{:S(2)}, u32[]{:S(2)}) %collective-permute-start.5) | collective-permute-done | bytes 278560 | tf_op jit(solution)/shard_map/ppermute | solution.py:518
  195.5 0.0 copy-done.9
  195.5 0.0 copy-done.4
  195.5 0.0 copy-done.5
  195.5 0.0 copy-done.10
  195.5 0.0 copy-done.12
  195.5 0.0 copy-done.14
  195.5 14.0 %shard_map.117 = bf16[1024,512]{1,0:T(8,128)(2,1)} custom-call(bf16[272,512]{1,0:T(8,128)(2,1)S(1)} %collective-permute-done.5.refs_0_.refs_1_, bf16[272,512]{1,0:T(8,128)(2,1)S(1)} %collective-permute-done.5.refs_0_.refs_1_, f32[3,512]{1,0:T(4,128)S(1)} %copy-done.12, bf16[3,512,512]{2,1,0:T(8,128)(2,1)S(1)} %copy-done.1, ...), custom_call_target="tpu_custom_call" | custom-call | flops 805306368 | bytes 13606912 | tf_op jit(solution)/shard_map/pallas_call | solution.py:459
Async XLA Ops:
  2.9 32.6 %collective-permute-start.1 = (bf16[400,512]{1,0:T(8,128)(2,1)}, bf16[400,512]{1,0:T(8,128)(2,1)}, u32[]{:S(2)}, u32[]{:S(2)}) collective-permute-start(bf16[400,512]{1,0:T(8,128)(2,1)} %shard_map.109.refs_7_), channel_id=1, source_target_pairs={{0,4},{1,5},{2,6},{3,7},{4,0},{5,1},{6,2},{7,3},{8,12},{9,13},{10,... | collective-permute-start | bytes 1228808 | tf_op jit(solution)/shard_map/ppermute | solution.py:518
  9.2 36.1 %collective-permute-start.2 = (bf16[224,512]{1,0:T(8,128)(2,1)}, bf16[224,512]{1,0:T(8,128)(2,1)}, u32[]{:S(2)}, u32[]{:S(2)}) collective-permute-start(bf16[224,512]{1,0:T(8,128)(2,1)} %get-tuple-element.33), channel_id=1, source_target_pairs={{0,4},{1,5},{2,6},{3,7},{4,0},{5,1},{6,2},{7,3},{8,12},{9,13},{10,... | collective-permute-start | bytes 688136 | tf_op jit(solution)/shard_map/ppermute | solution.py:518
  9.3 36.0 %collective-permute-start.3 = (bf16[224,512]{1,0:T(8,128)(2,1)}, bf16[224,512]{1,0:T(8,128)(2,1)}, u32[]{:S(2)}, u32[]{:S(2)}) collective-permute-start(bf16[224,512]{1,0:T(8,128)(2,1)} %get-tuple-element.34), channel_id=1, source_target_pairs={{0,4},{1,5},{2,6},{3,7},{4,0},{5,1},{6,2},{7,3},{8,12},{9,13},{10,... | collective-permute-start | bytes 688136 | tf_op jit(solution)/shard_map/ppermute | solution.py:518
  130.2 29.9 %collective-permute-start.4 = (bf16[528,512]{1,0:T(8,128)(2,1)}, bf16[528,512]{1,0:T(8,128)(2,1)S(1)}, u32[]{:S(2)}, u32[]{:S(2)}) collective-permute-start(bf16[528,512]{1,0:T(8,128)(2,1)} %get-tuple-element.44.refs_0_.refs_9_), channel_id=1, source_target_pairs={{0,8},{1,9},{2,10},{3,11},{4,12},{5,13},{6,14},{7,15},{8,0},{9,1},... | collective-permute-start | bytes 1622024 | tf_op jit(solution)/shard_map/ppermute | solution.py:518
  136.7 1.4 copy-start
  138.1 1.4 copy-start.2
  139.6 1.4 copy-start.7
  141.0 0.7 copy-start.11
  141.7 0.7 copy-start.13
  142.3 1.0 copy-start.15
  143.4 16.7 %copy-start.1 = (bf16[3,512,512]{2,1,0:T(8,128)(2,1)S(1)}, bf16[3,512,512]{2,1,0:T(8,128)(2,1)}, u32[]{:S(2)}) copy-start(bf16[3,512,512]{2,1,0:T(8,128)(2,1)} %refs_3_.11) | copy-start | bytes 4718596
  143.4 16.7 %copy-start.3 = (bf16[3,512,512]{2,1,0:T(8,128)(2,1)S(1)}, bf16[3,512,512]{2,1,0:T(8,128)(2,1)}, u32[]{:S(2)}) copy-start(bf16[3,512,512]{2,1,0:T(8,128)(2,1)} %refs_4_.9) | copy-start | bytes 4718596
  143.4 16.7 %copy-start.6 = (bf16[3,512,512]{2,1,0:T(8,128)(2,1)S(1)}, bf16[3,512,512]{2,1,0:T(8,128)(2,1)}, u32[]{:S(2)}) copy-start(bf16[3,512,512]{2,1,0:T(8,128)(2,1)} %refs_10_.5) | copy-start | bytes 4718596
  160.1 27.3 %copy-start.8 = (bf16[3,512,512]{2,1,0:T(8,128)(2,1)S(1)}, bf16[3,512,512]{2,1,0:T(8,128)(2,1)}, u32[]{:S(2)}) copy-start(bf16[3,512,512]{2,1,0:T(8,128)(2,1)} %refs_3_.10) | copy-start | bytes 4718596
  160.1 35.3 %copy-start.9 = (bf16[1024,512]{1,0:T(8,128)(2,1)S(1)}, bf16[1024,512]{1,0:T(8,128)(2,1)}, u32[]{:S(2)}) copy-start(bf16[1024,512]{1,0:T(8,128)(2,1)} %get-tuple-element.55.refs_15_) | copy-start | bytes 3145732
  186.8 8.7 %copy-start.4 = (bf16[512,2048]{1,0:T(8,128)(2,1)S(1)}, bf16[512,2048]{1,0:T(8,128)(2,1)}, u32[]{:S(2)}) copy-start(bf16[512,2048]{1,0:T(8,128)(2,1)} %refs_12_.1) | copy-start | bytes 6291460
  186.8 8.7 %copy-start.5 = (bf16[2048,512]{1,0:T(8,128)(2,1)S(1)}, bf16[2048,512]{1,0:T(8,128)(2,1)}, u32[]{:S(2)}) copy-start(bf16[2048,512]{1,0:T(8,128)(2,1)} %refs_13_.1) | copy-start | bytes 6291460
  186.8 8.7 %copy-start.10 = (f32[8,1024]{1,0:T(8,128)S(1)}, f32[8,1024]{1,0:T(8,128)}, u32[]{:S(2)}) copy-start(f32[8,1024]{1,0:T(8,128)} %get-tuple-element.43.refs_17_.refs_16_) | copy-start | bytes 98308
  186.8 8.7 %copy-start.12 = (f32[3,512]{1,0:T(4,128)S(1)}, f32[3,512]{1,0:T(4,128)}, u32[]{:S(2)}) copy-start(f32[3,512]{1,0:T(4,128)} %refs_2_.11) | copy-start | bytes 18436
  186.8 8.7 %copy-start.14 = (f32[512]{0:T(512)S(1)}, f32[512]{0:T(512)}, u32[]{:S(2)}) copy-start(f32[512]{0:T(512)} %param.21) | copy-start | bytes 6148
  186.8 8.6 %collective-permute-start.5 = (bf16[272,512]{1,0:T(8,128)(2,1)S(1)}, bf16[272,512]{1,0:T(8,128)(2,1)S(1)}, u32[]{:S(2)}, u32[]{:S(2)}) collective-permute-start(bf16[272,512]{1,0:T(8,128)(2,1)S(1)} %get-tuple-element.49.refs_0_.refs_9_), channel_id=1, source_target_pairs={{0,16},{1,17},{2,18},{3,19},{4,20},{5,21},{6,22},{7,23},{8,24},{9,... | collective-permute-start | bytes 835592 | tf_op jit(solution)/shard_map/ppermute | solution.py:518
where the time goes:
time: 213 us; the launch traced here: 210 us
  Pallas kernels  162 us (76%)
  waiting for transfers between devices  24.3 us (11%)
  starting transfers between devices  13.8 us (6%)
  local copies, waits for them, and re-layouts  7.9 us (4%)
    pallas_call x9, Pallas kernels, call(): pl.pallas_call(body, out_shape=outs, in_specs=[ANY if manual or i in raw...  162 us
    ppermute x5, waiting for transfers between devices, trade(): return lax.ppermute(value, 'leaf', [(s, s ^ 1 << bit) for s in range(size)])  24.3 us
    ppermute x5, starting transfers between devices, trade(): return lax.ppermute(value, 'leaf', [(s, s ^ 1 << bit) for s in range(size)])  13.8 us
    unnamed x32, local copies, waits for them, and re-layouts  6.7 us
  transfers between devices with their start and end apart: 5, of which 3 were waited for; matrix products, arithmetic and copies ran while one was open for 1% of the time, Pallas kernels for 16%

commit v1 on v0

--- a/solution.py
+++ b/solution.py
@@ -19,7 +19,7 @@
 ANY = pl.BlockSpec(memory_space=pl.ANY)
 VMEM = pl.BlockSpec(memory_space=pltpu.VMEM)
 FLAT = 1024 * 576
-SENT = (384, 224, 224, 192)
+SENT = (352, 240, 240, 192)
 USUAL = sum(SENT[:-1])
 EARLY = SENT[0]
 

time: 213 us -> 214 us (level)
  transfers between devices with their start and end apart: 5 -> 5, of which waited for: 3 -> 4; matrix products, arithmetic and copies ran while one was open for 1% -> 1% of each run, Pallas kernels for 16% -> 16%
where the time goes in v1:
time: 214 us; the launch traced here: 211 us
  Pallas kernels  163 us (76%)
  waiting for transfers between devices  24.9 us (12%)
  starting transfers between devices  14 us (7%)
  local copies, waits for them, and re-layouts  7.89 us (4%)
    pallas_call x9, Pallas kernels, call(): pl.pallas_call(body, out_shape=outs, in_specs=[ANY if manual or i in raw...  163 us
    ppermute x5, waiting for transfers between devices, trade(): return lax.ppermute(value, 'leaf', [(s, s ^ 1 << bit) for s in range(size)])  24.9 us
    ppermute x5, starting transfers between devices, trade(): return lax.ppermute(value, 'leaf', [(s, s ^ 1 << bit) for s in range(size)])  14 us
    unnamed x32, local copies, waits for them, and re-layouts  6.7 us
  transfers between devices with their start and end apart: 5, of which 4 were waited for; matrix products, arithmetic and copies ran while one was open for 1% of the time, Pallas kernels for 16%

profile of v1, /device:TPU:18, one launch (start us, length us, event | category | flops | bytes accessed | tf_op | source)
XLA Modules:
  0.0 210.7 jit_solution(4518983250873040398)
XLA Ops:
  0.0 2.8 %shard_map.109.refs_7_ = bf16[368,512]{1,0:T(8,128)(2,1)} custom-call(bf16[1024,512]{1,0:T(8,128)(2,1)} %refs_16_.1, s32[1,1024]{1,0:T(1,128)} %bitcast.4), custom_call_target="tpu_custom_call" | custom-call | flops 1000000000 | bytes 1429504 | tf_op jit(solution)/shard_map/pallas_call | solution.py:459
  2.8 3.4 %collective-permute-start.1 = (bf16[368,512]{1,0:T(8,128)(2,1)}, bf16[368,512]{1,0:T(8,128)(2,1)}, u32[]{:S(2)}, u32[]{:S(2)}) collective-permute-start(bf16[368,512]{1,0:T(8,128)(2,1)} %shard_map.109.refs_7_), channel_id=1, source_target_pairs={{0,4},{1,5},{2,6},{3,7},{4,0},{5,1},{6,2},{7,3},{8,12},{9,13},{10,... | collective-permute-start | bytes 1130504 | tf_op jit(solution)/shard_map/ppermute | solution.py:518
  6.2 3.0 %shard_map.110 = (bf16[240,512]{1,0:T(8,128)(2,1)}, bf16[240,512]{1,0:T(8,128)(2,1)}, bf16[192,512]{1,0:T(8,128)(2,1)}) custom-call(bf16[1024,512]{1,0:T(8,128)(2,1)} %refs_16_.1, s32[1,1024]{1,0:T(1,128)} %bitcast.5), custom_call_target="tpu_custom_call" | custom-call | flops 1000000000 | bytes 1740800 | tf_op jit(solution)/shard_map/pallas_call | solution.py:459
  9.2 0.1 collective-permute-start.2
  9.3 3.1 %collective-permute-start.3 = (bf16[240,512]{1,0:T(8,128)(2,1)}, bf16[240,512]{1,0:T(8,128)(2,1)}, u32[]{:S(2)}, u32[]{:S(2)}) collective-permute-start(bf16[240,512]{1,0:T(8,128)(2,1)} %get-tuple-element.34), channel_id=1, source_target_pairs={{0,4},{1,5},{2,6},{3,7},{4,0},{5,1},{6,2},{7,3},{8,12},{9,13},{10,... | collective-permute-start | bytes 737288 | tf_op jit(solution)/shard_map/ppermute | solution.py:518
  12.4 15.8 %shard_map.111 = (bf16[8,1024,128]{2,1,0:T(8,128)(2,1)}, f32[8,80,1024]{2,1,0:T(8,128)}, f32[16,128]{1,0:T(8,128)}, f32[16,128]{1,0:T(8,128)}, f32[8,1024]{1,0:T(8,128)}) custom-call(bf16[1024,512]{1,0:T(8,128)(2,1)} %refs_16_.1, s32[1,1024]{1,0:T(1,128)} %bitcast.6, f32[3,512]{1,0:T(4,128)} %refs_2_.11, bf16[3,512,512]{2,1,0:T(8,128)(2,1)} %refs_3_.10, ...), custom_call_target="tpu_custom_call" | custom-call | flops 8589934592 | bytes 10549248 | tf_op jit(solution)/shard_map/pallas_call | solution.py:459
  28.2 6.5 %collective-permute-done.1.refs_0_.refs_4_ = bf16[368,512]{1,0:T(8,128)(2,1)} collective-permute-done((bf16[368,512]{1,0:T(8,128)(2,1)}, bf16[368,512]{1,0:T(8,128)(2,1)}, u32[]{:S(2)}, u32[]{:S(2)}) %collective-permute-start.1) | collective-permute-done | bytes 376864 | tf_op jit(solution)/shard_map/ppermute | solution.py:518
  34.7 7.5 %shard_map.112 = (f32[8,80,1024]{2,1,0:T(8,128)}, f32[16,128]{1,0:T(8,128)}, s32[8,128]{1,0:T(8,128)}) custom-call(bf16[368,512]{1,0:T(8,128)(2,1)} %collective-permute-done.1.refs_0_.refs_4_, f32[3,512]{1,0:T(4,128)} %refs_2_.11, bf16[3,512,512]{2,1,0:T(8,128)(2,1)} %refs_3_.11, bf16[3,512,512]{2,1,0:T(8,128)(2,1)} %refs_4_.9, ...), custom_call_target="tpu_custom_call" | custom-call | flops 10000000000 | bytes 11266048 | tf_op jit(solution)/shard_map/pallas_call | solution.py:459
  42.2 1.2 slice.3
  44.0 0.3 conditional.1
  44.3 0.0 collective-permute-done.2.refs_1_.refs_5_
  44.3 0.1 collective-permute-done.3.refs_2_.refs_6_
  44.4 85.3 %shard_map.113 = (bf16[1024,512]{1,0:T(8,128)(2,1)}, bf16[528,512]{1,0:T(8,128)(2,1)}) custom-call(bf16[368,512]{1,0:T(8,128)(2,1)} %collective-permute-done.1.refs_0_.refs_4_, bf16[240,512]{1,0:T(8,128)(2,1)} %collective-permute-done.2.refs_1_.refs_5_, bf16[240,512]{1,0:T(8,128)(2,1)} %collective-permute-done.3.refs_2_.refs_6_, ...), custom_call_target="tpu_custom_call" | custom-call | flops 5100273664 | bytes 14264320 | tf_op jit(solution)/shard_map/pallas_call | solution.py:459
  129.8 6.8 %collective-permute-start.4 = (bf16[528,512]{1,0:T(8,128)(2,1)}, bf16[528,512]{1,0:T(8,128)(2,1)S(1)}, u32[]{:S(2)}, u32[]{:S(2)}) collective-permute-start(bf16[528,512]{1,0:T(8,128)(2,1)} %get-tuple-element.44.refs_0_.refs_9_), channel_id=1, source_target_pairs={{0,8},{1,9},{2,10},{3,11},{4,12},{5,13},{6,14},{7,15},{8,0},{9,1},... | collective-permute-start | bytes 1622024 | tf_op jit(solution)/shard_map/ppermute | solution.py:518
  136.6 0.0 copy-start
  136.6 1.4 copy-done
  138.0 0.0 copy-start.2
  138.0 1.4 copy-done.2
  139.4 0.0 copy-start.7
  139.4 1.4 copy-done.7
  140.8 0.0 copy-start.11
  140.8 0.7 copy-done.11
  141.5 0.0 copy-start.13
  141.5 0.7 copy-done.13
  142.2 0.0 copy-start.15
  142.2 1.0 copy-done.15
  143.2 0.0 copy-start.1
  143.2 0.0 copy-start.3
  143.2 0.0 copy-start.6
  143.2 4.6 %shard_map.114 = (bf16[8,512,128]{2,1,0:T(8,128)(2,1)S(1)}, f32[8,80,512]{2,1,0:T(8,128)S(1)}, f32[16,128]{1,0:T(8,128)S(1)}, f32[16,128]{1,0:T(8,128)S(1)}) custom-call(bf16[528,512]{1,0:T(8,128)(2,1)S(1)} %copy-done.15, s32[1,1024]{1,0:T(1,128)S(1)} %bitcast.8, f32[3,512]{1,0:T(4,128)S(1)} %copy-done.11, bf16[3,512,512]{2,1,0:T(8,128)(2,1)S(1)} %copy-done.7, ...), custom_call_target="tpu_custom_call" | custom-call | flops 2147483648 | bytes 7645184 | tf_op jit(solution)/shard_map/pallas_call | solution.py:459
  147.9 12.6 %collective-permute-done.4.refs_0_.refs_1_ = bf16[528,512]{1,0:T(8,128)(2,1)S(1)} collective-permute-done((bf16[528,512]{1,0:T(8,128)(2,1)}, bf16[528,512]{1,0:T(8,128)(2,1)S(1)}, u32[]{:S(2)}, u32[]{:S(2)}) %collective-permute-start.4) | collective-permute-done | bytes 540704 | tf_op jit(solution)/shard_map/ppermute | solution.py:518
  160.5 0.0 copy-done.1
  160.5 0.0 copy-done.3
  160.5 0.0 copy-done.6
  160.5 0.0 copy-start.8
  160.6 0.0 copy-start.9
  160.6 26.6 %shard_map.115 = (bf16[512,512]{1,0:T(8,128)(2,1)S(1)}, bf16[272,512]{1,0:T(8,128)(2,1)S(1)}) custom-call(bf16[528,512]{1,0:T(8,128)(2,1)S(1)} %collective-permute-done.4.refs_0_.refs_1_, bf16[528,512]{1,0:T(8,128)(2,1)S(1)} %collective-permute-done.4.refs_0_.refs_1_, f32[3,512]{1,0:T(4,128)S(1)} %copy-done.11, bf16[3,512,512]{2,1,0:T(8,128)(2,1)S(1)} %copy-done.1, ...), custom_call_target="tpu_custom_call" | custom-call | flops 2684354560 | bytes 9525248 | tf_op jit(solution)/shard_map/pallas_call | solution.py:459
  187.2 0.0 copy-start.4
  187.2 0.0 copy-start.5
  187.2 0.0 copy-start.10
  187.2 0.0 copy-start.12
  187.2 0.0 copy-start.14
  187.2 0.6 collective-permute-start.5
  187.9 0.0 copy-done.8
  187.9 3.0 %shard_map.116 = (bf16[8,256,128]{2,1,0:T(8,128)(2,1)S(1)}, f32[8,80,256]{2,1,0:T(8,128)S(1)}, f32[16,128]{1,0:T(8,128)S(1)}, f32[16,128]{1,0:T(8,128)S(1)}) custom-call(bf16[272,512]{1,0:T(8,128)(2,1)S(1)} %get-tuple-element.49.refs_0_.refs_9_, s32[1,1024]{1,0:T(1,128)S(1)} %bitcast.9, f32[3,512]{1,0:T(4,128)S(1)} %copy-done.11, ...), custom_call_target="tpu_custom_call" | custom-call | flops 536870912 | bytes 6203392 | tf_op jit(solution)/shard_map/pallas_call | solution.py:459
  190.9 5.6 %collective-permute-done.5.refs_0_.refs_1_ = bf16[272,512]{1,0:T(8,128)(2,1)S(1)} collective-permute-done((bf16[272,512]{1,0:T(8,128)(2,1)S(1)}, bf16[272,512]{1,0:T(8,128)(2,1)S(1)}, u32[]{:S(2)}, u32[]{:S(2)}) %collective-permute-start.5) | collective-permute-done | bytes 278560 | tf_op jit(solution)/shard_map/ppermute | solution.py:518
  196.5 0.0 copy-done.9
  196.5 0.0 copy-done.4
  196.5 0.0 copy-done.5
  196.5 0.0 copy-done.10
  196.5 0.0 copy-done.12
  196.5 0.0 copy-done.14
  196.5 14.0 %shard_map.117 = bf16[1024,512]{1,0:T(8,128)(2,1)} custom-call(bf16[272,512]{1,0:T(8,128)(2,1)S(1)} %collective-permute-done.5.refs_0_.refs_1_, bf16[272,512]{1,0:T(8,128)(2,1)S(1)} %collective-permute-done.5.refs_0_.refs_1_, f32[3,512]{1,0:T(4,128)S(1)} %copy-done.12, bf16[3,512,512]{2,1,0:T(8,128)(2,1)S(1)} %copy-done.1, ...), custom_call_target="tpu_custom_call" | custom-call | flops 805306368 | bytes 13606912 | tf_op jit(solution)/shard_map/pallas_call | solution.py:459
Async XLA Ops:
  2.8 31.9 %collective-permute-start.1 = (bf16[368,512]{1,0:T(8,128)(2,1)}, bf16[368,512]{1,0:T(8,128)(2,1)}, u32[]{:S(2)}, u32[]{:S(2)}) collective-permute-start(bf16[368,512]{1,0:T(8,128)(2,1)} %shard_map.109.refs_7_), channel_id=1, source_target_pairs={{0,4},{1,5},{2,6},{3,7},{4,0},{5,1},{6,2},{7,3},{8,12},{9,13},{10,... | collective-permute-start | bytes 1130504 | tf_op jit(solution)/shard_map/ppermute | solution.py:518
  9.2 35.2 %collective-permute-start.2 = (bf16[240,512]{1,0:T(8,128)(2,1)}, bf16[240,512]{1,0:T(8,128)(2,1)}, u32[]{:S(2)}, u32[]{:S(2)}) collective-permute-start(bf16[240,512]{1,0:T(8,128)(2,1)} %get-tuple-element.33), channel_id=1, source_target_pairs={{0,4},{1,5},{2,6},{3,7},{4,0},{5,1},{6,2},{7,3},{8,12},{9,13},{10,... | collective-permute-start | bytes 737288 | tf_op jit(solution)/shard_map/ppermute | solution.py:518
  9.3 35.1 %collective-permute-start.3 = (bf16[240,512]{1,0:T(8,128)(2,1)}, bf16[240,512]{1,0:T(8,128)(2,1)}, u32[]{:S(2)}, u32[]{:S(2)}) collective-permute-start(bf16[240,512]{1,0:T(8,128)(2,1)} %get-tuple-element.34), channel_id=1, source_target_pairs={{0,4},{1,5},{2,6},{3,7},{4,0},{5,1},{6,2},{7,3},{8,12},{9,13},{10,... | collective-permute-start | bytes 737288 | tf_op jit(solution)/shard_map/ppermute | solution.py:518
  129.8 30.8 %collective-permute-start.4 = (bf16[528,512]{1,0:T(8,128)(2,1)}, bf16[528,512]{1,0:T(8,128)(2,1)S(1)}, u32[]{:S(2)}, u32[]{:S(2)}) collective-permute-start(bf16[528,512]{1,0:T(8,128)(2,1)} %get-tuple-element.44.refs_0_.refs_9_), channel_id=1, source_target_pairs={{0,8},{1,9},{2,10},{3,11},{4,12},{5,13},{6,14},{7,15},{8,0},{9,1},... | collective-permute-start | bytes 1622024 | tf_op jit(solution)/shard_map/ppermute | solution.py:518
  136.6 1.4 copy-start
  138.0 1.4 copy-start.2
  139.4 1.4 copy-start.7
  140.8 0.7 copy-start.11
  141.5 0.7 copy-start.13
  142.2 1.0 copy-start.15
  143.2 17.3 %copy-start.1 = (bf16[3,512,512]{2,1,0:T(8,128)(2,1)S(1)}, bf16[3,512,512]{2,1,0:T(8,128)(2,1)}, u32[]{:S(2)}) copy-start(bf16[3,512,512]{2,1,0:T(8,128)(2,1)} %refs_3_.11) | copy-start | bytes 4718596
  143.2 17.3 %copy-start.3 = (bf16[3,512,512]{2,1,0:T(8,128)(2,1)S(1)}, bf16[3,512,512]{2,1,0:T(8,128)(2,1)}, u32[]{:S(2)}) copy-start(bf16[3,512,512]{2,1,0:T(8,128)(2,1)} %refs_4_.9) | copy-start | bytes 4718596
  143.2 17.3 %copy-start.6 = (bf16[3,512,512]{2,1,0:T(8,128)(2,1)S(1)}, bf16[3,512,512]{2,1,0:T(8,128)(2,1)}, u32[]{:S(2)}) copy-start(bf16[3,512,512]{2,1,0:T(8,128)(2,1)} %refs_10_.5) | copy-start | bytes 4718596
  160.5 27.3 %copy-start.8 = (bf16[3,512,512]{2,1,0:T(8,128)(2,1)S(1)}, bf16[3,512,512]{2,1,0:T(8,128)(2,1)}, u32[]{:S(2)}) copy-start(bf16[3,512,512]{2,1,0:T(8,128)(2,1)} %refs_3_.10) | copy-start | bytes 4718596
  160.6 35.9 %copy-start.9 = (bf16[1024,512]{1,0:T(8,128)(2,1)S(1)}, bf16[1024,512]{1,0:T(8,128)(2,1)}, u32[]{:S(2)}) copy-start(bf16[1024,512]{1,0:T(8,128)(2,1)} %get-tuple-element.55.refs_15_) | copy-start | bytes 3145732
  187.2 9.3 %copy-start.4 = (bf16[512,2048]{1,0:T(8,128)(2,1)S(1)}, bf16[512,2048]{1,0:T(8,128)(2,1)}, u32[]{:S(2)}) copy-start(bf16[512,2048]{1,0:T(8,128)(2,1)} %refs_12_.1) | copy-start | bytes 6291460
  187.2 9.3 %copy-start.5 = (bf16[2048,512]{1,0:T(8,128)(2,1)S(1)}, bf16[2048,512]{1,0:T(8,128)(2,1)}, u32[]{:S(2)}) copy-start(bf16[2048,512]{1,0:T(8,128)(2,1)} %refs_13_.1) | copy-start | bytes 6291460
  187.2 9.3 %copy-start.10 = (f32[8,1024]{1,0:T(8,128)S(1)}, f32[8,1024]{1,0:T(8,128)}, u32[]{:S(2)}) copy-start(f32[8,1024]{1,0:T(8,128)} %get-tuple-element.43.refs_17_.refs_16_) | copy-start | bytes 98308
  187.2 9.3 %copy-start.12 = (f32[3,512]{1,0:T(4,128)S(1)}, f32[3,512]{1,0:T(4,128)}, u32[]{:S(2)}) copy-start(f32[3,512]{1,0:T(4,128)} %refs_2_.11) | copy-start | bytes 18436
  187.2 9.3 %copy-start.14 = (f32[512]{0:T(512)S(1)}, f32[512]{0:T(512)}, u32[]{:S(2)}) copy-start(f32[512]{0:T(512)} %param.21) | copy-start | bytes 6148
  187.2 9.3 %collective-permute-start.5 = (bf16[272,512]{1,0:T(8,128)(2,1)S(1)}, bf16[272,512]{1,0:T(8,128)(2,1)S(1)}, u32[]{:S(2)}, u32[]{:S(2)}) collective-permute-start(bf16[272,512]{1,0:T(8,128)(2,1)S(1)} %get-tuple-element.49.refs_0_.refs_9_), channel_id=1, source_target_pairs={{0,16},{1,17},{2,18},{3,19},{4,20},{5,21},{6,22},{7,23},{8,24},{9,... | collective-permute-start | bytes 835592 | tf_op jit(solution)/shard_map/ppermute | solution.py:518
